TPU v7x, 512 devices: a whole 4x8x8 slice. The times are simulated.
512 devices in a mesh: section: 32 (over z_lo, y), tensor: 16 (over x, z_hi, core).
Axes of the slice: x: 4, y: 8, z: 8 (z_hi: 2, z_lo: 4; z = z_hi * 4 + z_lo), core: 2. Of those that a mesh axis runs over, the one named last changes fastest.
Arguments:
- vision_tokens: bfloat16 [2048, 1664], P('section'), may hold values from -6 to 6
- key_weight: bfloat16 [13312, 8192], P('section', 'tensor'), may hold values from -0.15625 to 0.15625
- value_weight: bfloat16 [13312, 8192], P('section', 'tensor'), may hold values from -0.15625 to 0.15625
- queries: bfloat16 [32, 1024, 8192], P('section', None, 'tensor'), may hold values from -6 to 6
- gate: float32 [8], replicated, may hold values from 0.3 to 1.5
- visible: int32 [4, 4, 4], replicated, may hold values from -1 to 1, as said below
- out_grad: bfloat16 [32, 1024, 8192], P('section', None, 'tensor'), may hold values from -6 to 6
Outputs:
- attended: bfloat16 [32, 1024, 8192], P('section', None, 'tensor')
- vision_grad: bfloat16 [2048, 1664], P('section')
Inputs may be any that keep to these rules, and one draw needn't show every extreme that they name: `visible`: each row of 4 entries is non-decreasing, and every image index 0 to 1 occurs in every row.
All inputs are finite; a program needn't handle non-finite values.
Results may differ from a plain program's by a relative error of at most 0.029.
Values may be sent and summed in bfloat16 or wider, within the bound.
A program may use at most 64 MiB of HBM per device.

v0:
```python
import jax
import jax.numpy as jnp
from jax import lax
from jax.sharding import PartitionSpec as P

HD = 128
IMG_TOK = 64
TBLOCK = 64
IMGS = 2
MICRO = 4


def from_partner(value, axis, distance):
    mask = 2**distance
    pairs = [(source, source ^ mask) for source in range(lax.axis_size(axis))]
    return lax.ppermute(value, axis, pairs)


def block_index(visible):
    samples = visible.shape[0]
    base = jnp.arange(samples, dtype=jnp.int32)[:, None] * IMGS
    seen = (base + jnp.maximum(visible, 0)).reshape(-1)
    validf = (visible >= 0).reshape(-1).astype(jnp.float32)
    return (seen, validf)


def local_layer(key_rows, value_rows, query, gate_value, cotangent, visible, heads):
    width = heads * HD
    seen, validf = block_index(visible)
    images = key_rows.shape[0] // IMG_TOK
    key_img = jnp.take(key_rows.reshape(images, IMG_TOK, heads, HD), seen, axis=0)
    val_img = jnp.take(value_rows.reshape(images, IMG_TOK, heads, HD), seen, axis=0)
    blocks = seen.shape[0]
    query_b = query.reshape(blocks, TBLOCK, heads, HD)
    scale = 1.0 / HD**0.5
    scores = (
        jnp.einsum("bqhd,bkhd->bhqk", query_b, key_img, preferred_element_type=jnp.float32) * scale
    )
    exponent = jnp.exp(scores)
    probs = exponent / jnp.sum(exponent, axis=-1, keepdims=True) * validf[:, None, None, None]
    probs_b = probs.astype(jnp.bfloat16)
    mixed = jnp.einsum("bhqk,bkhd->bqhd", probs_b, val_img, preferred_element_type=jnp.float32)
    factor = jnp.tanh(gate_value)
    attended = (factor * mixed).astype(jnp.bfloat16).reshape(-1, width)
    head_grad = (
        (factor * cotangent.astype(jnp.float32))
        .astype(jnp.bfloat16)
        .reshape(blocks, TBLOCK, heads, HD)
    )
    vgrad_blk = jnp.einsum(
        "bhqk,bqhd->bkhd", probs_b, head_grad, preferred_element_type=jnp.float32
    )
    prob_grad = jnp.einsum(
        "bqhd,bkhd->bhqk", head_grad, val_img, preferred_element_type=jnp.float32
    )
    delta = jnp.sum(probs * prob_grad, axis=-1, keepdims=True)
    score_grad = (probs * (prob_grad - delta) * scale).astype(jnp.bfloat16)
    kgrad_blk = jnp.einsum(
        "bhqk,bqhd->bkhd", score_grad, query_b, preferred_element_type=jnp.float32
    )
    onehot = (seen[:, None] == jnp.arange(images, dtype=jnp.int32)[None, :]).astype(jnp.float32)
    key_grad = (
        jnp.einsum("bi,bkhd->ikhd", onehot, kgrad_blk).reshape(-1, width).astype(jnp.bfloat16)
    )
    value_grad = (
        jnp.einsum("bi,bkhd->ikhd", onehot, vgrad_blk).reshape(-1, width).astype(jnp.bfloat16)
    )
    return (attended, key_grad, value_grad)


def back_product(grad_rows, weight):
    return lax.dot_general(
        grad_rows, weight, (((1,), (1,)), ((), ())), preferred_element_type=jnp.float32
    )


def upper_bit(position, bit):
    return position // 2**bit % 2 == 1


def join_pair(mine, partner, upper, axis):
    low_first = jnp.concatenate([mine, partner], axis=axis)
    high_first = jnp.concatenate([partner, mine], axis=axis)
    return jnp.where(upper, high_first, low_first)


def split_pair(values, upper):
    half = values.shape[0] // 2
    lower_rows = values[:half]
    upper_rows = values[half:]
    keep = jnp.where(upper, upper_rows, lower_rows)
    give = jnp.where(upper, lower_rows, upper_rows)
    return (keep, give)


def reduce_first(values, position, layer_bits):
    for bit in reversed(range(layer_bits)):
        keep, give = split_pair(values, upper_bit(position, bit))
        values = keep + from_partner(give.astype(jnp.bfloat16), "section", bit).astype(give.dtype)
    return values


def shards(vision_tokens, key_weight, value_weight, queries, gate, visible, out_grad):
    position = lax.axis_index("section")
    layers = lax.axis_size("section") // MICRO
    layer_bits = layers.bit_length() - 1
    layer = position % layers
    micro = position // layers
    stacked = jnp.stack([key_weight, value_weight])
    for offset in range(2):
        bit = layer_bits + offset
        partner = from_partner(stacked, "section", bit)
        stacked = join_pair(stacked, partner, upper_bit(position, bit), 1)
    w_key = stacked[0]
    w_value = stacked[1]
    width = w_key.shape[1]
    heads = width // HD
    gate_value = lax.dynamic_index_in_dim(gate, layer, 0, keepdims=False)
    own_visible = lax.dynamic_index_in_dim(visible, micro, 0, keepdims=False)
    all_rows = vision_tokens
    for bit in range(layer_bits):
        partner = from_partner(all_rows, "section", bit)
        all_rows = join_pair(all_rows, partner, upper_bit(position, bit), 0)
    key_rows = jnp.dot(all_rows, w_key, preferred_element_type=jnp.float32).astype(jnp.bfloat16)
    value_rows = jnp.dot(all_rows, w_value, preferred_element_type=jnp.float32).astype(jnp.bfloat16)
    attended, key_grad, value_grad = local_layer(
        key_rows, value_rows, queries[0], gate_value, out_grad[0], own_visible, heads
    )
    term = back_product(key_grad, w_key) + back_product(value_grad, w_value)
    summed = lax.psum(term.astype(jnp.bfloat16), "tensor").astype(jnp.float32)
    owned = reduce_first(summed, position, layer_bits).astype(jnp.bfloat16)
    return (attended[None], owned)


def solution(mesh):
    placed = (
        P("section", None),
        P("section", "tensor"),
        P("section", "tensor"),
        P("section", None, "tensor"),
        P(),
        P(),
        P("section", None, "tensor"),
    )
    return jax.shard_map(
        shards,
        mesh=mesh,
        in_specs=placed,
        out_specs=(P("section", None, "tensor"), P("section", None)),
        check_vma=False,
    )
```

profile of v0, /device:TPU:1, one launch (start us, length us, event | category | flops | bytes accessed | tf_op | source)
XLA Modules:
  0.0 440.8 jit_solution(11001433239776774613)
XLA Ops:
  8.5 5.0 %collective-permute-start.3 = (bf16[2,416,512]{2,1,0:T(8,128)(2,1)S(1)}, bf16[2,416,512]{2,1,0:T(8,128)(2,1)S(1)}, u32[]{:S(2)}, u32[]{:S(2)}) collective-permute-start(bf16[2,416,512]{2,1,0:T(8,128)(2,1)S(1)} %pad_maximum_fusion), channel_id=1, source_target_pairs={{0,128},{16,144},{32,160},{48,176},{64,192},{80,208},{96,224},{112... | collective-permute-start | bytes 2555912 | tf_op jit(solution)/shard_map/ppermute | solution.py:16
  13.5 14.5 %collective-permute-done.3 = bf16[2,416,512]{2,1,0:T(8,128)(2,1)S(1)} collective-permute-done((bf16[2,416,512]{2,1,0:T(8,128)(2,1)S(1)}, bf16[2,416,512]{2,1,0:T(8,128)(2,1)S(1)}, u32[]{:S(2)}, u32[]{:S(2)}) %collective-permute-start.3) | collective-permute-done | bytes 852000 | tf_op jit(solution)/shard_map/ppermute | solution.py:16
  30.0 9.9 %collective-permute-start.4 = (bf16[2,832,512]{2,1,0:T(8,128)(2,1)S(1)}, bf16[2,832,512]{2,1,0:T(8,128)(2,1)}, u32[]{:S(2)}, u32[]{:S(2)}) collective-permute-start(bf16[2,832,512]{2,1,0:T(8,128)(2,1)S(1)} %maximum_select_fusion.2), channel_id=1, source_target_pairs={{0,256},{16,272},{32,288},{48,304},{64,320},{80,336},{96,352},{112... | collective-permute-start | bytes 5111816 | tf_op jit(solution)/shard_map/ppermute | solution.py:16
  39.9 3.2 collective-permute-start
  44.8 2.3 collective-permute-done
  47.1 4.2 collective-permute-start.1
  52.8 16.9 %collective-permute-done.1 = bf16[128,1664]{1,0:T(8,128)(2,1)S(1)} collective-permute-done((bf16[128,1664]{1,0:T(8,128)(2,1)S(1)}, bf16[128,1664]{1,0:T(8,128)(2,1)S(1)}, u32[]{:S(2)}, u32[]{:S(2)}) %collective-permute-start.1) | collective-permute-done | bytes 426016 | tf_op jit(solution)/shard_map/ppermute | solution.py:16
  70.8 8.4 %collective-permute-start.2 = (bf16[256,1664]{1,0:T(8,128)(2,1)}, bf16[256,1664]{1,0:T(8,128)(2,1)}, u32[]{:S(2)}, u32[]{:S(2)}) collective-permute-start(bf16[256,1664]{1,0:T(8,128)(2,1)} %maximum_select_fusion.3), channel_id=1, source_target_pairs={{0,64},{16,80},{32,96},{48,112},{64,0},{80,16},{96,32},{112,48},{1... | collective-permute-start | bytes 2555912 | tf_op jit(solution)/shard_map/ppermute | solution.py:16
  79.3 2.1 reshape_squeeze.3
  82.6 30.7 %collective-permute-done.4 = bf16[2,832,512]{2,1,0:T(8,128)(2,1)} collective-permute-done((bf16[2,832,512]{2,1,0:T(8,128)(2,1)S(1)}, bf16[2,832,512]{2,1,0:T(8,128)(2,1)}, u32[]{:S(2)}, u32[]{:S(2)}) %collective-permute-start.4) | collective-permute-done | bytes 1703968 | tf_op jit(solution)/shard_map/ppermute | solution.py:16
  113.3 3.9 maximum_select_fusion
  117.2 3.9 fusion.19
  125.0 3.9 fusion.18
  132.9 2.7 gather_fusion
  135.6 2.7 gather_fusion.1
  138.3 2.5 bitcast_reduce_fusion
  144.5 6.1 %fusion.12 = bf16[16,4,64,128]{3,2,1,0:T(8,128)(2,1)} fusion(f32[16,4,64,64]{2,3,1,0:T(8,128)} %fusion.32, bf16[16,64,4,128]{3,2,1,0:T(4,128)(2,1)} %reshape_squeeze.3, f32[16,4,64,64]{3,2,1,0:T(8,128)} %copy-done.7, f32[16]{0:T(128)S(1)} %reshape.64, f32[16,4,64]{2,1,0:T(4,128)S(1)} %get-tuple-element.5), kind=kOutput, calls=%fused_computation.20 | convolution fusion | flops 69996608 | bytes 4210752 | tf_op jit(solution)/shard_map/bhqk,bqhd->bkhd/dot_general | solution.py:58
  156.1 2.4 add_convert_fusion
  158.5 196.9 %all-reduce.2.cloned.1.call-done = bf16[512,1664]{1,0:T(8,128)(2,1)} async-done(((bf16[512,1664]{1,0:T(8,128)(2,1)}), bf16[512,1664]{1,0:T(8,128)(2,1)}) %all-reduce.2.cloned.1.call-update) | async-done | bytes 1703952 | tf_op jit(solution)/shard_map/psum | solution.py:130
  357.3 7.2 %collective-permute-start.5 = (bf16[256,1664]{1,0:T(8,128)(2,1)S(1)}, bf16[256,1664]{1,0:T(8,128)(2,1)S(1)}, u32[]{:S(2)}, u32[]{:S(2)}) collective-permute-start(bf16[256,1664]{1,0:T(8,128)(2,1)S(1)} %select_convert_fusion), channel_id=1, source_target_pairs={{0,64},{16,80},{32,96},{48,112},{64,0},{80,16},{96,32},{112,48},{1... | collective-permute-start | bytes 2555912 | tf_op jit(solution)/shard_map/ppermute | solution.py:16
  364.5 29.0 %collective-permute-done.5 = bf16[256,1664]{1,0:T(8,128)(2,1)S(1)} collective-permute-done((bf16[256,1664]{1,0:T(8,128)(2,1)S(1)}, bf16[256,1664]{1,0:T(8,128)(2,1)S(1)}, u32[]{:S(2)}, u32[]{:S(2)}) %collective-permute-start.5) | collective-permute-done | bytes 852000 | tf_op jit(solution)/shard_map/ppermute | solution.py:16
  393.8 13.0 %collective-permute-start.6 = (bf16[128,1664]{1,0:T(8,128)(2,1)S(1)}, bf16[128,1664]{1,0:T(8,128)(2,1)S(1)}, u32[]{:S(2)}, u32[]{:S(2)}) collective-permute-start(bf16[128,1664]{1,0:T(8,128)(2,1)S(1)} %select_convert_fusion.1), channel_id=1, source_target_pairs={{0,32},{16,48},{32,0},{48,16},{64,96},{80,112},{96,64},{112,80},{1... | collective-permute-start | bytes 1277960 | tf_op jit(solution)/shard_map/ppermute | solution.py:16
  406.8 18.7 %collective-permute-done.6 = bf16[128,1664]{1,0:T(8,128)(2,1)S(1)} collective-permute-done((bf16[128,1664]{1,0:T(8,128)(2,1)S(1)}, bf16[128,1664]{1,0:T(8,128)(2,1)S(1)}, u32[]{:S(2)}, u32[]{:S(2)}) %collective-permute-start.6) | collective-permute-done | bytes 426016 | tf_op jit(solution)/shard_map/ppermute | solution.py:16
  430.7 2.6 collective-permute-done.7
  (60 shorter events, 33.0 us)
Async XLA Ops:
  7.2 348.3 %all-reduce.2.cloned.1.call-start = ((), (), s32[]{:S(2)}) async-start(), calls=%async_computation | async-start | bytes 3407872 | tf_op jit(solution)/shard_map/psum | solution.py:130
  8.4 31.5 %copy-start.4 = (bf16[64,1664]{1,0:T(8,128)(2,1)S(1)}, bf16[64,1664]{1,0:T(8,128)(2,1)}, u32[]{:S(2)}) copy-start(bf16[64,1664]{1,0:T(8,128)(2,1)} %param.9) | copy-start | bytes 638980
  8.4 34.8 %copy-start.6 = (f32[8]{0:T(128)S(1)}, f32[8]{0:T(128)}, u32[]{:S(2)}) copy-start(f32[8]{0:T(128)} %param.13) | copy-start | bytes 100
  8.5 36.2 %copy-start.5 = (s32[4,4,4]{2,1,0:T(4,128)S(1)}, s32[4,4,4]{2,1,0:T(4,128)}, u32[]{:S(2)}) copy-start(s32[4,4,4]{2,1,0:T(4,128)} %param.14) | copy-start | bytes 772
  8.5 19.5 %collective-permute-start.3 = (bf16[2,416,512]{2,1,0:T(8,128)(2,1)S(1)}, bf16[2,416,512]{2,1,0:T(8,128)(2,1)S(1)}, u32[]{:S(2)}, u32[]{:S(2)}) collective-permute-start(bf16[2,416,512]{2,1,0:T(8,128)(2,1)S(1)} %pad_maximum_fusion), channel_id=1, source_target_pairs={{0,128},{16,144},{32,160},{48,176},{64,192},{80,208},{96,224},{112... | collective-permute-start | bytes 2555912 | tf_op jit(solution)/shard_map/ppermute | solution.py:16
  29.9 40.8 %copy-start = (bf16[2,832,512]{2,1,0:T(8,128)(2,1)}, bf16[2,832,512]{2,1,0:T(8,128)(2,1)S(1)}, u32[]{:S(2)}) copy-start(bf16[2,832,512]{2,1,0:T(8,128)(2,1)S(1)} %maximum_select_fusion.2) | copy-start | bytes 5111812
  30.0 83.3 %collective-permute-start.4 = (bf16[2,832,512]{2,1,0:T(8,128)(2,1)S(1)}, bf16[2,832,512]{2,1,0:T(8,128)(2,1)}, u32[]{:S(2)}, u32[]{:S(2)}) collective-permute-start(bf16[2,832,512]{2,1,0:T(8,128)(2,1)S(1)} %maximum_select_fusion.2), channel_id=1, source_target_pairs={{0,256},{16,272},{32,288},{48,304},{64,320},{80,336},{96,352},{112... | collective-permute-start | bytes 5111816 | tf_op jit(solution)/shard_map/ppermute | solution.py:16
  39.9 7.1 %collective-permute-start = (bf16[64,1664]{1,0:T(8,128)(2,1)S(1)}, bf16[64,1664]{1,0:T(8,128)(2,1)S(1)}, u32[]{:S(2)}, u32[]{:S(2)}) collective-permute-start(bf16[64,1664]{1,0:T(8,128)(2,1)S(1)} %copy-done.4), channel_id=1, source_target_pairs={{0,16},{16,0},{32,48},{48,32},{64,80},{80,64},{96,112},{112,96},{1... | collective-permute-start | bytes 638984 | tf_op jit(solution)/shard_map/ppermute | solution.py:16
  47.1 22.6 %collective-permute-start.1 = (bf16[128,1664]{1,0:T(8,128)(2,1)S(1)}, bf16[128,1664]{1,0:T(8,128)(2,1)S(1)}, u32[]{:S(2)}, u32[]{:S(2)}) collective-permute-start(bf16[128,1664]{1,0:T(8,128)(2,1)S(1)} %maximum_select_fusion.4), channel_id=1, source_target_pairs={{0,32},{16,48},{32,0},{48,16},{64,96},{80,112},{96,64},{112,80},{1... | collective-permute-start | bytes 1277960 | tf_op jit(solution)/shard_map/ppermute | solution.py:16
  70.8 46.4 %collective-permute-start.2 = (bf16[256,1664]{1,0:T(8,128)(2,1)}, bf16[256,1664]{1,0:T(8,128)(2,1)}, u32[]{:S(2)}, u32[]{:S(2)}) collective-permute-start(bf16[256,1664]{1,0:T(8,128)(2,1)} %maximum_select_fusion.3), channel_id=1, source_target_pairs={{0,64},{16,80},{32,96},{48,112},{64,0},{80,16},{96,32},{112,48},{1... | collective-permute-start | bytes 2555912 | tf_op jit(solution)/shard_map/ppermute | solution.py:16
  138.3 2.5 copy-start.1
  138.3 2.5 copy-start.3
  140.8 2.1 copy-start.7
  357.3 36.2 %collective-permute-start.5 = (bf16[256,1664]{1,0:T(8,128)(2,1)S(1)}, bf16[256,1664]{1,0:T(8,128)(2,1)S(1)}, u32[]{:S(2)}, u32[]{:S(2)}) collective-permute-start(bf16[256,1664]{1,0:T(8,128)(2,1)S(1)} %select_convert_fusion), channel_id=1, source_target_pairs={{0,64},{16,80},{32,96},{48,112},{64,0},{80,16},{96,32},{112,48},{1... | collective-permute-start | bytes 2555912 | tf_op jit(solution)/shard_map/ppermute | solution.py:16
  393.8 33.9 %copy-start.2 = (bf16[16,64,4,128]{3,1,2,0:T(8,128)(2,1)S(1)}, bf16[16,64,4,128]{3,1,2,0:T(8,128)(2,1)}, u32[]{:S(2)}) copy-start(bf16[16,64,4,128]{3,1,2,0:T(8,128)(2,1)} %gather_fusion) | copy-start | bytes 3145732
  393.8 33.9 %copy-start.8 = (f32[16,4,64,64]{3,2,1,0:T(8,128)S(1)}, f32[16,4,64,64]{3,2,1,0:T(8,128)}, u32[]{:S(2)}) copy-start(f32[16,4,64,64]{3,2,1,0:T(8,128)} %copy-done.7) | copy-start | bytes 3145732
  393.8 31.8 %collective-permute-start.6 = (bf16[128,1664]{1,0:T(8,128)(2,1)S(1)}, bf16[128,1664]{1,0:T(8,128)(2,1)S(1)}, u32[]{:S(2)}, u32[]{:S(2)}) collective-permute-start(bf16[128,1664]{1,0:T(8,128)(2,1)S(1)} %select_convert_fusion.1), channel_id=1, source_target_pairs={{0,32},{16,48},{32,0},{48,16},{64,96},{80,112},{96,64},{112,80},{1... | collective-permute-start | bytes 1277960 | tf_op jit(solution)/shard_map/ppermute | solution.py:16
  425.7 7.5 %collective-permute-start.7 = (bf16[64,1664]{1,0:T(8,128)(2,1)S(1)}, bf16[64,1664]{1,0:T(8,128)(2,1)S(1)}, u32[]{:S(2)}, u32[]{:S(2)}) collective-permute-start(bf16[64,1664]{1,0:T(8,128)(2,1)S(1)} %select_convert_fusion.2), channel_id=1, source_target_pairs={{0,16},{16,0},{32,48},{48,32},{64,80},{80,64},{96,112},{112,96},{1... | collective-permute-start | bytes 638984 | tf_op jit(solution)/shard_map/ppermute | solution.py:16
Sparse Core Ops, SparseCore 0:
  158.7 196.7 all-reduce.1
where the time goes:
time: 442 us; the launch traced here: 441 us
  waiting for transfers between devices  312 us (71%)
  starting transfers between devices  52.9 us (12%)
  matrix products  28.4 us (6%)
  local copies, waits for them, and re-layouts  20 us (5%)
  between operations  15.2 us (3%)
  other arithmetic  12.7 us (3%)
    psum x1, waiting for transfers between devices, shards(): summed = lax.psum(term.astype(jnp.bfloat16), 'tensor').astype(jnp.float32)  197 us
    ppermute x8, waiting for transfers between devices, from_partner(): return lax.ppermute(value, axis, pairs)  115 us
    ppermute x8, starting transfers between devices, from_partner(): return lax.ppermute(value, axis, pairs)  52.8 us
  transfers between devices with their start and end apart: 9, of which 8 were waited for; matrix products, arithmetic and copies ran while one was open for 3% of the time, Pallas kernels for 0%

commit v1 on v0

v1 whole, which is shorter than its diff:
```python
import jax
import jax.numpy as jnp
from jax import lax
from jax.experimental import pallas as pl
from jax.experimental.pallas import tpu as pltpu
from jax.sharding import PartitionSpec as P

HD = 128
NZ, NY, NX = 4, 8, 4
HEADS = 4
SAMPLES = 4
QB = 416
DV = 1664
VT = 512
SHARE = 896
STEP = 768
CH = 4
PER = NY // CH
SCALE = 1.0 / HD**0.5
MESH = pl.DeviceIdType.MESH
F32 = jnp.float32
BF16 = jnp.bfloat16


def nt(a, b):
    return lax.dot_general(a, b, (((1,), (1,)), ((), ())), preferred_element_type=F32)


def nn(a, b):
    return lax.dot_general(a, b, (((1,), (0,)), ((), ())), preferred_element_type=F32)


def tn(a, b):
    return lax.dot_general(a, b, (((0,), (0,)), ((), ())), preferred_element_type=F32)


def kernel(
    gate, visible, vision, wk, wv, query, cot, att_out, vis_out,
    wbuf, xbuf, qbuf, gbuf, abuf, bias, kvbuf, dkv, acc,
    s1, r1, xs, xr, ys, yr, zs, zr, fs, ar, obuf,
    lsem, lw, lq, lg, lo,
    zsend, zrecv, xsend, xrecv, xsib,
    s1s, s1r, b2s, b2r, b3s, b3r, b4s, b4r, b5s, b5r,
):
    section = lax.axis_index("section")
    tensor = lax.axis_index("tensor")
    p = section // NY
    y = section % NY
    x = tensor // 4
    zh = (tensor // 2) % 2
    c = tensor % 2
    sib = (section, tensor + 1 - 2 * c)

    def at_y(d):
        return (p * NY + lax.rem(y + d, NY), tensor)

    def at_x(d, core):
        return (section, lax.rem(x + d, NX) * 4 + zh * 2 + core)

    partner = (section, x * 4 + (1 - zh) * 2 + c)

    own_x = pltpu.make_async_copy(vision, xbuf.at[pl.ds(y * 64, 64)], lsem.at[0])
    own_x.start()

    def local_w(h, kv):
        ref = wv if kv else wk
        return pltpu.make_async_copy(
            ref.at[:, pl.ds(h * HD, HD)],
            wbuf.at[h, pl.ds(p * QB, QB), pl.ds(kv * HD, HD)],
            lw.at[h, kv],
        )

    for h in range(HEADS):
        local_w(h, 0).start()
        local_w(h, 1).start()

    def local_q(h):
        return pltpu.make_async_copy(query.at[0, :, pl.ds(h * HD, HD)], qbuf.at[h], lq.at[h])

    def local_g(h):
        return pltpu.make_async_copy(cot.at[0, :, pl.ds(h * HD, HD)], gbuf.at[h], lg.at[h])

    for h in range(HEADS):
        local_q(h).start()
        local_g(h).start()

    barrier = pltpu.get_barrier_semaphore()

    def greet(device):
        pl.semaphore_signal(barrier, inc=1, device_id=device, device_id_type=MESH)

    has_left = p > 0
    has_right = p < NZ - 1

    @pl.when(has_left)
    def _():
        greet((section - NY, tensor))

    @pl.when(has_right)
    def _():
        greet((section + NY, tensor))

    for d in range(1, NY):
        greet(at_y(d))
    for d in range(1, NX):
        greet(at_x(d, c))
    for d in range(NX):
        greet(at_x(d, 1 - c))
    greet(partner)
    ends = jnp.where(has_left, 1, 0) + jnp.where(has_right, 1, 0)
    pl.semaphore_wait(barrier, 15 + ends)

    def zcopy(q, h, right):
        rows = pl.ds(pl.multiple_of(q * QB, 16), QB)
        return pltpu.make_async_remote_copy(
            src_ref=wbuf.at[h, rows],
            dst_ref=wbuf.at[h, rows],
            send_sem=zsend.at[right, q, h],
            recv_sem=zrecv.at[q, h],
            device_id=(section + (NY if right else -NY), tensor),
            device_id_type=MESH,
        )

    for h in range(HEADS):
        local_w(h, 0).wait()
        local_w(h, 1).wait()

        @pl.when(has_left)
        def _():
            zcopy(p, h, 0).start()

        @pl.when(has_right)
        def _():
            zcopy(p, h, 1).start()

    def xcopy(source, to, core):
        rows = pl.ds(pl.multiple_of(source * 64 + core * 32, 32), 32)
        return pltpu.make_async_remote_copy(
            src_ref=xbuf.at[rows],
            dst_ref=xbuf.at[rows],
            send_sem=xsend.at[to, source],
            recv_sem=xsib.at[source] if to == 2 else xrecv.at[source],
            device_id=(at_y(1), at_y(NY - 1), sib)[to],
            device_id_type=MESH,
        )

    own_x.wait()
    xcopy(y, 0, c).start()
    xcopy(y, 1, c).start()

    lane = lax.broadcasted_iota(jnp.int32, (128, 256), 1)
    image = lax.broadcasted_iota(jnp.int32, (128, 256), 0) // 64
    for s in range(SAMPLES):
        seen = jnp.where(
            lane < 128,
            jnp.where(lane < 64, visible[p, s, 0], visible[p, s, 1]),
            jnp.where(lane < 192, visible[p, s, 2], visible[p, s, 3]),
        )
        bias[s] = jnp.where(seen == image, 0.0, -1e30).astype(F32)
    acc[...] = jnp.zeros_like(acc)

    for t in range(1, 5):
        below = lax.rem(y + NY - t, NY)
        xcopy(below, 0, c).wait_recv()
        if t < 4:
            xcopy(below, 0, c).start()
        xcopy(below, 2, c).start()
        if t < 4:
            above = lax.rem(y + t, NY)
            xcopy(above, 1, c).wait_recv()
            if t < 3:
                xcopy(above, 1, c).start()
            xcopy(above, 2, c).start()
    for t in range(1, NY):
        source = lax.rem(y + t, NY)
        xcopy(source, 2, 1 - c).wait_recv()
    factor = jnp.tanh(jnp.full((1, HD), gate[y], F32))

    def one_head(h, carry):
        for d in range(1, NZ):

            @pl.when(p + d < NZ)
            def _():
                q = p + d
                zcopy(q, h, 0).wait_recv()

                @pl.when(has_left)
                def _():
                    zcopy(q, h, 0).start()

            @pl.when(p - d >= 0)
            def _():
                q = p - d
                zcopy(q, h, 1).wait_recv()

                @pl.when(has_right)
                def _():
                    zcopy(q, h, 1).start()

        local_q(h).wait()
        local_g(h).wait()
        kvbuf[...] = nn(xbuf[...], wbuf[h]).astype(BF16)
        for s in range(SAMPLES):
            keys = kvbuf[pl.ds(s * 128, 128), :HD]
            values = kvbuf[pl.ds(s * 128, 128), HD:]
            qs = qbuf[h, pl.ds(s * 256, 256)]
            hg = (factor * gbuf[h, pl.ds(s * 256, 256)].astype(F32)).astype(BF16)
            e = jnp.exp(nt(keys, qs) * SCALE + bias[s])
            total = jnp.sum(e, axis=0, keepdims=True)
            probs = e * (1.0 / jnp.where(total > 0.0, total, 1.0))
            probs_b = probs.astype(BF16)
            abuf[h, pl.ds(s * 256, 256)] = (factor * tn(probs_b, values)).astype(BF16)
            dkv[pl.ds(s * 128, 128), HD:] = nn(probs_b, hg).astype(BF16)
            pg = nt(values, hg)
            delta = jnp.sum(probs * pg, axis=0, keepdims=True)
            sg = (probs * (pg - delta) * SCALE).astype(BF16)
            dkv[pl.ds(s * 128, 128), :HD] = nn(sg, qs).astype(BF16)
        out_copy(h).start()
        acc[...] += nt(dkv[...], wbuf[h])
        return carry

    def out_copy(h):
        return pltpu.make_async_copy(abuf.at[h], att_out.at[0, :, pl.ds(h * HD, HD)], lo.at[h])

    lax.fori_loop(0, HEADS, one_head, 0)

    def b1(k):
        return pltpu.make_async_remote_copy(
            src_ref=s1.at[k], dst_ref=r1.at[k], send_sem=s1s.at[k], recv_sem=s1r.at[k],
            device_id=sib, device_id_type=MESH,
        )

    for k in range(CH):
        for j in range(PER):
            o = k + CH * j
            start = pl.multiple_of(o * 64 + (1 - c) * 32, 32)
            s1[k, j] = acc[pl.ds(start, 32)].astype(BF16)
        b1(k).start()

    def b2(k, d):
        peer = lax.rem(x + d, NX)
        row = pl.multiple_of((peer // 2) * 16, 16)
        col = pl.multiple_of((peer % 2) * STEP, 128)
        return pltpu.make_async_remote_copy(
            src_ref=xs.at[k, :, pl.ds(row, 16), pl.ds(col, SHARE)],
            dst_ref=xr.at[k, d - 1],
            send_sem=b2s.at[k, d - 1], recv_sem=b2r.at[k, d - 1],
            device_id=at_x(d, c), device_id_type=MESH,
        )

    for k in range(CH):
        b1(k).wait_recv()
        for j in range(PER):
            o = k + CH * j
            start = pl.multiple_of(o * 64 + c * 32, 32)
            xs[k, j] = (acc[pl.ds(start, 32)] + r1[k, j].astype(F32)).astype(BF16)
        for d in (2, 1, 3):
            b2(k, d).start()

    my_row = pl.multiple_of((x // 2) * 16, 16)
    my_col = pl.multiple_of((x % 2) * STEP, 128)

    def b3(k, j):
        return pltpu.make_async_remote_copy(
            src_ref=ys.at[k, j], dst_ref=yr.at[y],
            send_sem=b3s.at[k, j], recv_sem=b3r.at[y],
            device_id=(p * NY + k + CH * j, tensor), device_id_type=MESH,
        )

    for k in range(CH):
        for d in range(1, NX):
            b2(k, d).wait_recv()
        part = xs[k, :, pl.ds(my_row, 16), pl.ds(my_col, SHARE)].astype(F32)
        for d in range(NX - 1):
            part = part + xr[k, d].astype(F32)
        ys[k] = part.astype(BF16)
        for j in range(PER):

            @pl.when(y != k + CH * j)
            def _():
                b3(k, j).start()

    total = ys[y % CH, y // CH].astype(F32)
    for d in range(1, NY):
        source = lax.rem(y + d, NY)
        pltpu.make_async_remote_copy(
            src_ref=ys.at[0, 0], dst_ref=yr.at[source],
            send_sem=b3s.at[0, 0], recv_sem=b3r.at[source],
            device_id=at_y(d), device_id_type=MESH,
        ).wait_recv()
        total = total + yr[source].astype(F32)
    zs[...] = total.astype(BF16)
    b4 = pltpu.make_async_remote_copy(
        src_ref=zs, dst_ref=zr, send_sem=b4s, recv_sem=b4r, device_id=partner, device_id_type=MESH
    )
    b4.start()
    b4.wait_recv()
    fs[...] = (zs[...].astype(F32) + zr[...].astype(F32)).astype(BF16)

    def b5(d, other):
        core = 1 - c if other else c
        return pltpu.make_async_remote_copy(
            src_ref=fs, dst_ref=ar.at[c, x],
            send_sem=b5s.at[other, d], recv_sem=b5r.at[c, x],
            device_id=at_x(d, core), device_id_type=MESH,
        )

    everyone = [(d, o) for d in (2, 1, 3, 0) for o in (0, 1) if (d, o) != (0, 0)]
    for d, o in everyone:
        b5(d, o).start()
    ar[c, x] = fs[...]
    for d, o in everyone:
        core = 1 - c if o else c
        source = lax.rem(x + d, NX)
        pltpu.make_async_remote_copy(
            src_ref=fs, dst_ref=ar.at[core, source],
            send_sem=b5s.at[o, d], recv_sem=b5r.at[core, source],
            device_id=at_x(d, core), device_id_type=MESH,
        ).wait_recv()
    for core in range(2):
        for i in range(2):
            rows = pl.ds(core * 32 + i * 16, 16)
            obuf[rows, pl.ds(0, SHARE)] = ar[core, 2 * i]
            obuf[rows, pl.ds(SHARE, DV - SHARE)] = ar[core, 2 * i + 1, :, pl.ds(SHARE - STEP, DV - SHARE)]
    last = pltpu.make_async_copy(obuf, vis_out, lsem.at[1])
    last.start()

    for h in range(HEADS):
        for q in range(NZ):

            @pl.when(jnp.logical_and(has_left, p <= q))
            def _():
                zcopy(q, h, 0).wait_send()

            @pl.when(jnp.logical_and(has_right, p >= q))
            def _():
                zcopy(q, h, 1).wait_send()

    xcopy(y, 0, c).wait_send()
    xcopy(y, 1, c).wait_send()
    for t in range(1, 5):
        below = lax.rem(y + NY - t, NY)
        if t < 4:
            xcopy(below, 0, c).wait_send()
        xcopy(below, 2, c).wait_send()
        if t < 4:
            above = lax.rem(y + t, NY)
            if t < 3:
                xcopy(above, 1, c).wait_send()
            xcopy(above, 2, c).wait_send()
    for k in range(CH):
        b1(k).wait_send()
        for d in range(1, NX):
            b2(k, d).wait_send()
        for j in range(PER):

            @pl.when(y != k + CH * j)
            def _():
                b3(k, j).wait_send()

    b4.wait_send()
    for d, o in everyone:
        b5(d, o).wait_send()
    for h in range(HEADS):
        out_copy(h).wait()
    last.wait()


def shards(vision_tokens, key_weight, value_weight, queries, gate, visible, out_grad):
    dma = pltpu.SemaphoreType.DMA
    hbm = pl.BlockSpec(memory_space=pl.ANY)
    smem = pl.BlockSpec(memory_space=pltpu.SMEM)
    return pl.pallas_call(
        kernel,
        out_shape=(
            jax.ShapeDtypeStruct(queries.shape, BF16),
            jax.ShapeDtypeStruct(vision_tokens.shape, BF16),
        ),
        in_specs=[smem, smem, hbm, hbm, hbm, hbm, hbm],
        out_specs=(hbm, hbm),
        scratch_shapes=[
            pltpu.VMEM((HEADS, DV, 2 * HD), BF16),
            pltpu.VMEM((VT, DV), BF16),
            pltpu.VMEM((HEADS, 1024, HD), BF16),
            pltpu.VMEM((HEADS, 1024, HD), BF16),
            pltpu.VMEM((HEADS, 1024, HD), BF16),
            pltpu.VMEM((SAMPLES, 128, 256), F32),
            pltpu.VMEM((VT, 2 * HD), BF16),
            pltpu.VMEM((VT, 2 * HD), BF16),
            pltpu.VMEM((VT, DV), F32),
            pltpu.VMEM((CH, PER, 32, DV), BF16),
            pltpu.VMEM((CH, PER, 32, DV), BF16),
            pltpu.VMEM((CH, PER, 32, DV), BF16),
            pltpu.VMEM((CH, NX - 1, PER, 16, SHARE), BF16),
            pltpu.VMEM((CH, PER, 16, SHARE), BF16),
            pltpu.VMEM((NY, 16, SHARE), BF16),
            pltpu.VMEM((16, SHARE), BF16),
            pltpu.VMEM((16, SHARE), BF16),
            pltpu.VMEM((16, SHARE), BF16),
            pltpu.VMEM((2, NX, 16, SHARE), BF16),
            pltpu.VMEM((64, DV), BF16),
            dma((2,)),
            dma((HEADS, 2)),
            dma((HEADS,)),
            dma((HEADS,)),
            dma((HEADS,)),
            dma((2, NZ, HEADS)),
            dma((NZ, HEADS)),
            dma((3, NY)),
            dma((NY,)),
            dma((NY,)),
            dma((CH,)),
            dma((CH,)),
            dma((CH, NX - 1)),
            dma((CH, NX - 1)),
            dma((CH, PER)),
            dma((NY,)),
            dma,
            dma,
            dma((2, NX)),
            dma((2, NX)),
        ],
        compiler_params=pltpu.CompilerParams(
            collective_id=0, has_side_effects=True, vmem_limit_bytes=48 * 2**20
        ),
        cost_estimate=pl.CostEstimate(flops=4 * 10**9, bytes_accessed=5 * 10**6, transcendentals=2**19),
    )(gate, visible, vision_tokens, key_weight, value_weight, queries, out_grad)


def solution(mesh):
    placed = (
        P("section", None),
        P("section", "tensor"),
        P("section", "tensor"),
        P("section", None, "tensor"),
        P(),
        P(),
        P("section", None, "tensor"),
    )
    return jax.shard_map(
        shards,
        mesh=mesh,
        in_specs=placed,
        out_specs=(P("section", None, "tensor"), P("section", None)),
        check_vma=False,
    )
```

time: 442 us -> 114 us (0.26)
  the two profiles are of different devices: /device:TPU:1 before, /device:TPU:57 now
where the time goes in v1:
time: 114 us
  Pallas kernels  105 us (92%)
  local copies, waits for them, and re-layouts  8.39 us (7%)
    pallas_call x1, Pallas kernels, shards(): pl.pallas_call(kernel, out_shape=(jax.ShapeDtypeStruct(queries.shape, BF1...  105 us
    unnamed x16, local copies, waits for them, and re-layouts  8.39 us

profile of v1, /device:TPU:57, one launch (start us, length us, event | category | flops | bytes accessed | tf_op | source)
XLA Modules:
  0.0 114.1 jit_solution(9523338961506860730)
XLA Ops:
  0.6 0.0 copy-start
  0.6 1.2 %copy-done = bf16[1,1024,512]{2,1,0:T(8,128)(2,1)S(1)} copy-done((bf16[1,1024,512]{2,1,0:T(8,128)(2,1)S(1)}, bf16[1,1024,512]{2,1,0:T(8,128)(2,1)}, u32[]{:S(2)}) %copy-start) | copy-done | bytes 1048600
  1.9 0.0 copy-start.1
  1.9 1.2 %copy-done.1 = bf16[1,1024,512]{2,1,0:T(8,128)(2,1)S(1)} copy-done((bf16[1,1024,512]{2,1,0:T(8,128)(2,1)S(1)}, bf16[1,1024,512]{2,1,0:T(8,128)(2,1)}, u32[]{:S(2)}) %copy-start.1) | copy-done | bytes 1048600
  3.1 0.0 copy-start.2
  3.1 1.0 copy-done.2
  4.1 0.0 copy-start.3
  4.1 1.0 copy-done.3
  5.1 0.0 copy-start.4
  5.1 0.9 copy-done.4
  6.0 0.0 copy-start.5
  6.0 0.7 copy-done.5
  6.7 0.0 copy-start.6
  6.7 0.7 copy-done.6
  7.4 105.1 %shard_map.86 = (bf16[1,1024,512]{2,1,0:T(8,128)(2,1)S(1)}, bf16[64,1664]{1,0:T(8,128)(2,1)S(1)}) custom-call(f32[8]{0:T(128)S(1)} %copy-done.6, s32[4,4,4]{2,1,0:T(4,128)S(1)} %copy-done.5, bf16[64,1664]{1,0:T(8,128)(2,1)S(1)} %copy-done.4, bf16[416,512]{1,0:T(8,128)(2,1)S(1)} %copy-done.2, bf16[416,512]{1,0:T(8,128)(2,1)S(1)} %copy-done.3, ...), custom_call_target="tpu_custom_call" | custom-call | flops 4000000000 | bytes 5000000 | tf_op jit(solution)/shard_map/pallas_call | solution.py:373
  112.4 1.0 copy.11
  113.4 0.7 copy.12
Async XLA Ops:
  0.6 1.2 %copy-start = (bf16[1,1024,512]{2,1,0:T(8,128)(2,1)S(1)}, bf16[1,1024,512]{2,1,0:T(8,128)(2,1)}, u32[]{:S(2)}) copy-start(bf16[1,1024,512]{2,1,0:T(8,128)(2,1)} %query.1) | copy-start | bytes 3145732
  1.9 1.2 %copy-start.1 = (bf16[1,1024,512]{2,1,0:T(8,128)(2,1)S(1)}, bf16[1,1024,512]{2,1,0:T(8,128)(2,1)}, u32[]{:S(2)}) copy-start(bf16[1,1024,512]{2,1,0:T(8,128)(2,1)} %cot.1) | copy-start | bytes 3145732
  3.1 1.0 copy-start.2
  4.1 1.0 copy-start.3
  5.1 0.9 copy-start.4
  6.0 0.7 copy-start.5
  6.7 0.7 copy-start.6

commit v2 on v1

v2 whole, which is shorter than its diff:
```python
import jax
import jax.numpy as jnp
from jax import lax
from jax.experimental import pallas as pl
from jax.experimental.pallas import tpu as pltpu
from jax.sharding import PartitionSpec as P

HD = 128
NZ, NY, NX = 4, 8, 4
HEADS = 4
SAMPLES = 4
QB = 416
DV = 1664
VT = 512
SHARE = 896
STEP = 768
SCALE = 1.0 / HD**0.5
MESH = pl.DeviceIdType.MESH
F32 = jnp.float32
BF16 = jnp.bfloat16


def nt(a, b):
    return lax.dot_general(a, b, (((1,), (1,)), ((), ())), preferred_element_type=F32)


def nn(a, b):
    return lax.dot_general(a, b, (((1,), (0,)), ((), ())), preferred_element_type=F32)


def tn(a, b):
    return lax.dot_general(a, b, (((0,), (0,)), ((), ())), preferred_element_type=F32)


def reduction(acc, bufs, sems, place, peers):
    s1, r1, xs, xr, ys, yr, zs, zr, fs, ar = bufs
    sent, sent_all, got_pair, got_x, got_y, got_plane, got_all = sems
    section, p, y, x, c = place
    sib, partner, at_y, at_x = peers
    everyone = [(d, o) for d in (2, 1, 3, 0) for o in (0, 1) if (d, o) != (0, 0)]
    my_row = pl.multiple_of((x // 2) * 16, 16)
    my_col = pl.multiple_of((x % 2) * STEP, 128)

    def remote(src, dst, send, recv, device):
        return pltpu.make_async_remote_copy(
            src_ref=src, dst_ref=dst, send_sem=send, recv_sem=recv, device_id=device, device_id_type=MESH
        )

    def half(k, j, core):
        return pl.ds(pl.multiple_of((sample_at(y, k) * 2 + j) * 64 + core * 32, 32), 32)

    def b1(k):
        return remote(s1.at[k], r1.at[k], sent.at[k, 0], got_pair.at[k], sib)

    def pair(k):
        for j in range(2):
            s1[k, j] = acc[half(k, j, 1 - c)].astype(BF16)
        b1(k).start()

    def b2(k, d):
        peer = lax.rem(x + d, NX)
        row = pl.multiple_of((peer // 2) * 16, 16)
        col = pl.multiple_of((peer % 2) * STEP, 128)
        return remote(
            xs.at[k, :, pl.ds(row, 16), pl.ds(col, SHARE)], xr.at[k, d - 1],
            sent.at[k, d], got_x.at[k, d - 1], at_x(d, c),
        )

    def along_x(k):
        b1(k).wait_recv()
        for j in range(2):
            xs[k, j] = (acc[half(k, j, c)] + r1[k, j].astype(F32)).astype(BF16)
        for d in (2, 1, 3):
            b2(k, d).start()

    def b3(k, j):
        owner = (p * NY + sample_at(y, k) * 2 + j, lax.axis_index("tensor"))
        return remote(ys.at[k, j], yr.at[y], sent.at[k, 4 + j], got_y.at[y], owner)

    def owners(k):
        return (0, 1) if k < SAMPLES - 1 else (1 - y % 2,)

    def along_y(k):
        for d in range(1, NX):
            b2(k, d).wait_recv()
        total = xs[k, :, pl.ds(my_row, 16), pl.ds(my_col, SHARE)].astype(F32)
        for d in range(NX - 1):
            total = total + xr[k, d].astype(F32)
        ys[k] = total.astype(BF16)
        for j in owners(k):
            b3(k, j).start()

    def b4():
        return remote(zs, zr, sent_all.at[0], got_plane, partner)

    def planes():
        total = ys[SAMPLES - 1, y % 2].astype(F32)
        for d in (4, 3, 5, 2, 6, 1, 7):
            source = lax.rem(y + d, NY)
            remote(ys.at[0, 0], yr.at[source], sent.at[0, 4], got_y.at[source], at_y(d)).wait_recv()
            total = total + yr[source].astype(F32)
        zs[...] = total.astype(BF16)
        b4().start()

    def b5(d, other, core, source):
        return remote(
            fs, ar.at[core, source], sent_all.at[d * 2 + other], got_all.at[core, source],
            at_x(d, 1 - c if other else c),
        )

    def spread():
        b4().wait_recv()
        fs[...] = (zs[...].astype(F32) + zr[...].astype(F32)).astype(BF16)
        for d, o in everyone:
            b5(d, o, c, x).start()
        ar[c, x] = fs[...]

    def collect(out):
        for d, o in everyone:
            b5(d, o, 1 - c if o else c, lax.rem(x + d, NX)).wait_recv()
        for core in range(2):
            for i in range(2):
                rows = pl.ds(core * 32 + i * 16, 16)
                out[rows, pl.ds(0, SHARE)] = ar[core, 2 * i]
                out[rows, pl.ds(SHARE, DV - SHARE)] = ar[core, 2 * i + 1, :, pl.ds(SHARE - STEP, DV - SHARE)]

    def all_sent():
        for k in range(SAMPLES):
            b1(k).wait_send()
            for d in range(1, NX):
                b2(k, d).wait_send()
            for j in owners(k):
                b3(k, j).wait_send()
        b4().wait_send()
        for d, o in everyone:
            b5(d, o, c, x).wait_send()

    return dict(
        pair=pair, along_x=along_x, along_y=along_y, planes=planes, spread=spread, collect=collect, sent=all_sent
    )


def sample_at(y, k):
    return lax.rem(y // 2 + 1 + k, SAMPLES)


def reduction_bufs():
    shapes = [(SAMPLES, 2, 32, DV)] * 3 + [(SAMPLES, NX - 1, 2, 16, SHARE), (SAMPLES, 2, 16, SHARE)]
    shapes += [(NY, 16, SHARE)] + [(16, SHARE)] * 3 + [(2, NX, 16, SHARE)]
    return [pltpu.VMEM(shape, BF16) for shape in shapes]


def reduction_sems():
    dma = pltpu.SemaphoreType.DMA
    shapes = [(SAMPLES, 6), (8,), (SAMPLES,), (SAMPLES, NX - 1), (NY,)]
    return [dma(shape) for shape in shapes] + [dma, dma((2, NX))]


def kernel(
    gate, visible, vision, wk, wv, query, cot, att_out, vis_out,
    wbuf, xbuf, qbuf, gbuf, abuf, bias, kvbuf, dkv, acc,
    obuf, bufs, lsem, lw, lq, lg, lo, zsend, zrecv, xsend, xrecv, xsib, sems,
):
    section = lax.axis_index("section")
    tensor = lax.axis_index("tensor")
    p = section // NY
    y = section % NY
    x = tensor // 4
    zh = (tensor // 2) % 2
    c = tensor % 2
    sib = (section, tensor + 1 - 2 * c)

    def at_y(d):
        return (p * NY + lax.rem(y + d, NY), tensor)

    def at_x(d, core):
        return (section, lax.rem(x + d, NX) * 4 + zh * 2 + core)

    partner = (section, x * 4 + (1 - zh) * 2 + c)

    own_x = pltpu.make_async_copy(vision, xbuf.at[pl.ds(y * 64, 64)], lsem.at[0])
    own_x.start()

    def local_w(h, kv):
        ref = wv if kv else wk
        return pltpu.make_async_copy(
            ref.at[:, pl.ds(h * HD, HD)],
            wbuf.at[h, pl.ds(p * QB, QB), pl.ds(kv * HD, HD)],
            lw.at[h, kv],
        )

    for h in range(HEADS):
        local_w(h, 0).start()
        local_w(h, 1).start()

    def local_q(h):
        return pltpu.make_async_copy(query.at[0, :, pl.ds(h * HD, HD)], qbuf.at[h], lq.at[h])

    def local_g(h):
        return pltpu.make_async_copy(cot.at[0, :, pl.ds(h * HD, HD)], gbuf.at[h], lg.at[h])

    for h in range(HEADS):
        local_q(h).start()
        local_g(h).start()

    barrier = pltpu.get_barrier_semaphore()

    def greet(device):
        pl.semaphore_signal(barrier, inc=1, device_id=device, device_id_type=MESH)

    has_left = p > 0
    has_right = p < NZ - 1

    @pl.when(has_left)
    def _():
        greet((section - NY, tensor))

    @pl.when(has_right)
    def _():
        greet((section + NY, tensor))

    for d in range(1, NY):
        greet(at_y(d))
    for d in range(1, NX):
        greet(at_x(d, c))
    for d in range(NX):
        greet(at_x(d, 1 - c))
    greet(partner)
    ends = jnp.where(has_left, 1, 0) + jnp.where(has_right, 1, 0)
    pl.semaphore_wait(barrier, 15 + ends)

    def zcopy(q, h, right):
        rows = pl.ds(pl.multiple_of(q * QB, 16), QB)
        return pltpu.make_async_remote_copy(
            src_ref=wbuf.at[h, rows],
            dst_ref=wbuf.at[h, rows],
            send_sem=zsend.at[right, q, h],
            recv_sem=zrecv.at[q, h],
            device_id=(section + (NY if right else -NY), tensor),
            device_id_type=MESH,
        )

    for h in range(HEADS):
        local_w(h, 0).wait()
        local_w(h, 1).wait()

        @pl.when(has_left)
        def _():
            zcopy(p, h, 0).start()

        @pl.when(has_right)
        def _():
            zcopy(p, h, 1).start()

    def relay(d, h):
        @pl.when(p + d < NZ)
        def _():
            q = p + d
            zcopy(q, h, 0).wait_recv()

            @pl.when(has_left)
            def _():
                zcopy(q, h, 0).start()

        @pl.when(p - d >= 0)
        def _():
            q = p - d
            zcopy(q, h, 1).wait_recv()

            @pl.when(has_right)
            def _():
                zcopy(q, h, 1).start()

    def xcopy(source, to, core):
        rows = pl.ds(pl.multiple_of(source * 64 + core * 32, 32), 32)
        return pltpu.make_async_remote_copy(
            src_ref=xbuf.at[rows],
            dst_ref=xbuf.at[rows],
            send_sem=xsend.at[to, source],
            recv_sem=xsib.at[source] if to == 2 else xrecv.at[source],
            device_id=(at_y(1), at_y(NY - 1), sib)[to],
            device_id_type=MESH,
        )

    own_x.wait()
    xcopy(y, 0, c).start()
    xcopy(y, 1, c).start()

    lane = lax.broadcasted_iota(jnp.int32, (128, 256), 1)
    image = lax.broadcasted_iota(jnp.int32, (128, 256), 0) // 64
    for s in range(SAMPLES):
        seen = jnp.where(
            lane < 128,
            jnp.where(lane < 64, visible[p, s, 0], visible[p, s, 1]),
            jnp.where(lane < 192, visible[p, s, 2], visible[p, s, 3]),
        )
        bias[s] = jnp.where(seen == image, 0.0, -1e30).astype(F32)
    acc[...] = jnp.zeros_like(acc)

    for t in range(1, 5):
        below = lax.rem(y + NY - t, NY)
        xcopy(below, 0, c).wait_recv()
        if t < 4:
            xcopy(below, 0, c).start()
        xcopy(below, 2, c).start()
        if t < 4:
            above = lax.rem(y + t, NY)
            xcopy(above, 1, c).wait_recv()
            if t < 3:
                xcopy(above, 1, c).start()
            xcopy(above, 2, c).start()
        relay(1, t - 1)
    for t in range(1, NY):
        source = lax.rem(y + t, NY)
        xcopy(source, 2, 1 - c).wait_recv()
    factor = jnp.tanh(jnp.full((1, HD), gate[y], F32))

    def ready(h):
        for d in range(2, NZ):
            relay(d, h)
        local_q(h).wait()
        local_g(h).wait()
        kvbuf[...] = nn(xbuf[...], wbuf[h]).astype(BF16)

    def attend(h, s):
        image_rows = pl.ds(pl.multiple_of(s * 128, 128), 128)
        text_rows = pl.ds(pl.multiple_of(s * 256, 256), 256)
        keys = kvbuf[image_rows, :HD]
        values = kvbuf[image_rows, HD:]
        qs = qbuf[h, text_rows]
        hg = (factor * gbuf[h, text_rows].astype(F32)).astype(BF16)
        e = jnp.exp(nt(keys, qs) * SCALE + bias[s])
        total = jnp.sum(e, axis=0, keepdims=True)
        probs = e * (1.0 / jnp.where(total > 0.0, total, 1.0))
        probs_b = probs.astype(BF16)
        abuf[h, text_rows] = (factor * tn(probs_b, values)).astype(BF16)
        dkv[image_rows, HD:] = nn(probs_b, hg).astype(BF16)
        pg = nt(values, hg)
        delta = jnp.sum(probs * pg, axis=0, keepdims=True)
        sg = (probs * (pg - delta) * SCALE).astype(BF16)
        dkv[image_rows, :HD] = nn(sg, qs).astype(BF16)

    def one_head(h, carry):
        ready(h)
        for s in range(SAMPLES):
            attend(h, s)
        out_copy(h).start()
        acc[...] += nt(dkv[...], wbuf[h])
        return carry

    def out_copy(h):
        return pltpu.make_async_copy(abuf.at[h], att_out.at[0, :, pl.ds(h * HD, HD)], lo.at[h])

    lax.fori_loop(0, HEADS - 1, one_head, 0)

    reduce = reduction(acc, bufs, sems, (section, p, y, x, c), (sib, partner, at_y, at_x))
    ready(HEADS - 1)
    for k in range(SAMPLES):
        s = sample_at(y, k)
        attend(HEADS - 1, s)
        rows = pl.ds(pl.multiple_of(s * 128, 128), 128)
        acc[rows] += nt(dkv[rows], wbuf[HEADS - 1])
        reduce["pair"](k)
        if k:
            reduce["along_x"](k - 1)
    reduce["along_x"](SAMPLES - 1)
    out_copy(HEADS - 1).start()
    for k in range(SAMPLES):
        reduce["along_y"](k)
    reduce["planes"]()
    reduce["spread"]()
    reduce["collect"](obuf)
    last = pltpu.make_async_copy(obuf, vis_out, lsem.at[1])
    last.start()

    for h in range(HEADS):
        for q in range(NZ):

            @pl.when(jnp.logical_and(has_left, p <= q))
            def _():
                zcopy(q, h, 0).wait_send()

            @pl.when(jnp.logical_and(has_right, p >= q))
            def _():
                zcopy(q, h, 1).wait_send()

    xcopy(y, 0, c).wait_send()
    xcopy(y, 1, c).wait_send()
    for t in range(1, 5):
        below = lax.rem(y + NY - t, NY)
        if t < 4:
            xcopy(below, 0, c).wait_send()
        xcopy(below, 2, c).wait_send()
        if t < 4:
            above = lax.rem(y + t, NY)
            if t < 3:
                xcopy(above, 1, c).wait_send()
            xcopy(above, 2, c).wait_send()
    reduce["sent"]()
    for h in range(HEADS):
        out_copy(h).wait()
    last.wait()


def shards(vision_tokens, key_weight, value_weight, queries, gate, visible, out_grad):
    dma = pltpu.SemaphoreType.DMA
    hbm = pl.BlockSpec(memory_space=pltpu.HBM)
    smem = pl.BlockSpec(memory_space=pltpu.SMEM)
    return pl.pallas_call(
        kernel,
        out_shape=(
            jax.ShapeDtypeStruct(queries.shape, BF16),
            jax.ShapeDtypeStruct(vision_tokens.shape, BF16),
        ),
        in_specs=[smem, smem, hbm, hbm, hbm, hbm, hbm],
        out_specs=(pl.BlockSpec(memory_space=pl.ANY),) * 2,
        scratch_shapes=[
            pltpu.VMEM((HEADS, DV, 2 * HD), BF16),
            pltpu.VMEM((VT, DV), BF16),
            pltpu.VMEM((HEADS, 1024, HD), BF16),
            pltpu.VMEM((HEADS, 1024, HD), BF16),
            pltpu.VMEM((HEADS, 1024, HD), BF16),
            pltpu.VMEM((SAMPLES, 128, 256), F32),
            pltpu.VMEM((VT, 2 * HD), BF16),
            pltpu.VMEM((VT, 2 * HD), BF16),
            pltpu.VMEM((VT, DV), F32),
            pltpu.VMEM((64, DV), BF16),
            reduction_bufs(),
            dma((2,)),
            dma((HEADS, 2)),
            dma((HEADS,)),
            dma((HEADS,)),
            dma((HEADS,)),
            dma((2, NZ, HEADS)),
            dma((NZ, HEADS)),
            dma((3, NY)),
            dma((NY,)),
            dma((NY,)),
            reduction_sems(),
        ],
        compiler_params=pltpu.CompilerParams(
            collective_id=0, has_side_effects=True, vmem_limit_bytes=60 * 2**20
        ),
        cost_estimate=pl.CostEstimate(flops=4 * 10**9, bytes_accessed=5 * 10**6, transcendentals=2**19),
    )(gate, visible, vision_tokens, key_weight, value_weight, queries, out_grad)


def solution(mesh):
    placed = (
        P("section", None),
        P("section", "tensor"),
        P("section", "tensor"),
        P("section", None, "tensor"),
        P(),
        P(),
        P("section", None, "tensor"),
    )
    return jax.shard_map(
        shards,
        mesh=mesh,
        in_specs=placed,
        out_specs=(P("section", None, "tensor"), P("section", None)),
        check_vma=False,
    )
```

time: 114 us -> 106 us (0.930)
  the two profiles are of different devices: /device:TPU:57 before, /device:TPU:1 now
where the time goes in v2:
time: 106 us; the launch traced here: 105 us
  Pallas kernels  102 us (96%)
  local copies, waits for them, and re-layouts  2.99 us (3%)
    pallas_call x1, Pallas kernels, shards(): pl.pallas_call(kernel, out_shape=(jax.ShapeDtypeStruct(queries.shape, BF1...  102 us
    unnamed x4, local copies, waits for them, and re-layouts  2.99 us

profile of v2, /device:TPU:1, one launch (start us, length us, event | category | flops | bytes accessed | tf_op | source)
XLA Modules:
  0.0 105.4 jit_solution(8464566439521345482)
XLA Ops:
  0.6 101.8 %shard_map.86 = (bf16[1,1024,512]{2,1,0:T(8,128)(2,1)}, bf16[64,1664]{1,0:T(8,128)(2,1)}) custom-call(f32[8]{0:T(128)} %gate.1, s32[4,4,4]{2,1,0:T(4,128)} %visible.1, bf16[64,1664]{1,0:T(8,128)(2,1)} %vision.1, bf16[416,512]{1,0:T(8,128)(2,1)} %wk.1, bf16[416,512]{1,0:T(8,128)(2,1)} %wv.1, bf16[1,1024,512]{2,1,0:T(8,128)(2,1)} %query.1, ...), custom_call_target="tpu_custom_call" | custom-call | flops 4000000000 | bytes 5000000 | tf_op jit(solution)/shard_map/pallas_call | solution.py:409
  102.4 0.0 copy-start
  102.4 2.3 %copy.11 = bf16[1,1024,512]{2,1,0:T(8,128)(2,1)} copy(bf16[1,1024,512]{2,1,0:T(8,128)(2,1)} %get-tuple-element.4) | data formatting | bytes 2097152
  104.7 0.0 copy-done
  104.7 0.7 copy.12
Async XLA Ops:
  102.4 2.3 %copy-start = (bf16[64,1664]{1,0:T(8,128)(2,1)S(1)}, bf16[64,1664]{1,0:T(8,128)(2,1)}, u32[]{:S(2)}) copy-start(bf16[64,1664]{1,0:T(8,128)(2,1)} %get-tuple-element.5) | copy-start | bytes 638980

commit v3 on v2

--- a/solution.py
+++ b/solution.py
@@ -93,13 +93,16 @@
     def b4():
         return remote(zs, zr, sent_all.at[0], got_plane, partner)
 
-    def planes():
+    def owned():
         total = ys[SAMPLES - 1, y % 2].astype(F32)
         for d in (4, 3, 5, 2, 6, 1, 7):
             source = lax.rem(y + d, NY)
             remote(ys.at[0, 0], yr.at[source], sent.at[0, 4], got_y.at[source], at_y(d)).wait_recv()
             total = total + yr[source].astype(F32)
-        zs[...] = total.astype(BF16)
+        return total
+
+    def planes(more):
+        zs[...] = (owned() + more[...].astype(F32)).astype(BF16)
         b4().start()
 
     def b5(d, other, core, source):
@@ -124,19 +127,23 @@
                 out[rows, pl.ds(0, SHARE)] = ar[core, 2 * i]
                 out[rows, pl.ds(SHARE, DV - SHARE)] = ar[core, 2 * i + 1, :, pl.ds(SHARE - STEP, DV - SHARE)]
 
-    def all_sent():
+    def shared_sent():
         for k in range(SAMPLES):
             b1(k).wait_send()
             for d in range(1, NX):
                 b2(k, d).wait_send()
             for j in owners(k):
                 b3(k, j).wait_send()
+
+    def all_sent():
+        shared_sent()
         b4().wait_send()
         for d, o in everyone:
             b5(d, o, c, x).wait_send()
 
     return dict(
-        pair=pair, along_x=along_x, along_y=along_y, planes=planes, spread=spread, collect=collect, sent=all_sent
+        pair=pair, along_x=along_x, along_y=along_y, planes=planes, spread=spread, collect=collect, sent=all_sent,
+        owned=owned, shared_sent=shared_sent,
     )
 
 
@@ -159,7 +166,8 @@
 def kernel(
     gate, visible, vision, wk, wv, query, cot, att_out, vis_out,
     wbuf, xbuf, qbuf, gbuf, abuf, bias, kvbuf, dkv, acc,
-    obuf, bufs, lsem, lw, lq, lg, lo, zsend, zrecv, xsend, xrecv, xsib, sems,
+    xbuf2, qbuf2, gbuf2, abuf2, bias2, acc2, mine2, more,
+    obuf, bufs, bufs2, lsem, lw, lq, lg, lo, zsend, zrecv, xsems, xsems2, msend, mrecv, sems, sems2,
 ):
     section = lax.axis_index("section")
     tensor = lax.axis_index("tensor")
@@ -210,6 +218,28 @@
 
     has_left = p > 0
     has_right = p < NZ - 1
+    inner = jnp.logical_and(has_left, has_right)
+    end = jnp.logical_or(p == 0, p == NZ - 1)
+    mate = section + NY - 2 * NY * (p % 2)
+
+    def to_mate(i, src, dst):
+        return pltpu.make_async_remote_copy(
+            src_ref=src, dst_ref=dst, send_sem=msend.at[i], recv_sem=mrecv.at[i],
+            device_id=(mate, tensor), device_id_type=MESH,
+        )
+
+    own_half = pl.ds(pl.multiple_of(y * 64 + c * 32, 32), 32)
+
+    def lend(i):
+        if i == 0:
+            return to_mate(0, xbuf.at[own_half], xbuf2.at[own_half])
+        return to_mate(1, qbuf.at[0], qbuf2.at[0]) if i == 1 else to_mate(2, gbuf.at[0], gbuf2.at[0])
+
+    def give_back():
+        return to_mate(3, abuf2.at[0], abuf.at[0])
+
+    def give_sum():
+        return to_mate(4, mine2, more)
 
     @pl.when(has_left)
     def _():
@@ -240,120 +270,225 @@
             device_id_type=MESH,
         )
 
+    def send_left(h):
+        return p > (1 if h == 0 else 0)
+
+    def send_right(h):
+        return p < (NZ - 2 if h == 0 else NZ - 1)
+
     for h in range(HEADS):
         local_w(h, 0).wait()
         local_w(h, 1).wait()
 
-        @pl.when(has_left)
+        @pl.when(send_left(h))
         def _():
             zcopy(p, h, 0).start()
 
-        @pl.when(has_right)
+        @pl.when(send_right(h))
         def _():
             zcopy(p, h, 1).start()
 
-    def relay(d, h):
-        @pl.when(p + d < NZ)
+        if h == 0:
+            own_x.wait()
+
+            @pl.when(end)
+            def _():
+                lend(0).start()
+
+        if h == 2:
+            local_q(0).wait()
+            local_g(0).wait()
+
+            @pl.when(end)
+            def _():
+                lend(1).start()
+                lend(2).start()
+
+    def relay(d, h, takes):
+        relay_sides(d, h, takes, takes)
+
+    def relay_sides(d, h, from_right, from_left):
+        @pl.when(jnp.logical_and(from_right, p + d < NZ))
         def _():
             q = p + d
             zcopy(q, h, 0).wait_recv()
 
-            @pl.when(has_left)
+            @pl.when(send_left(h))
             def _():
                 zcopy(q, h, 0).start()
 
-        @pl.when(p - d >= 0)
+        @pl.when(jnp.logical_and(from_left, p - d >= 0))
         def _():
             q = p - d
             zcopy(q, h, 1).wait_recv()
 
-            @pl.when(has_right)
+            @pl.when(send_right(h))
             def _():
                 zcopy(q, h, 1).start()
 
-    def xcopy(source, to, core):
+    def xcopy(source, to, core, buf=xbuf, xs=xsems):
         rows = pl.ds(pl.multiple_of(source * 64 + core * 32, 32), 32)
+        sent, ring, side = xs
         return pltpu.make_async_remote_copy(
-            src_ref=xbuf.at[rows],
-            dst_ref=xbuf.at[rows],
-            send_sem=xsend.at[to, source],
-            recv_sem=xsib.at[source] if to == 2 else xrecv.at[source],
+            src_ref=buf.at[rows],
+            dst_ref=buf.at[rows],
+            send_sem=sent.at[to, source],
+            recv_sem=side.at[source] if to == 2 else ring.at[source],
             device_id=(at_y(1), at_y(NY - 1), sib)[to],
             device_id_type=MESH,
         )
 
-    own_x.wait()
+    def xcopy2(source, to, core):
+        return xcopy(source, to, core, xbuf2, xsems2)
+
+    def step(t, copy):
+        below = lax.rem(y + NY - t, NY)
+        copy(below, 0, c).wait_recv()
+        if t < 4:
+            copy(below, 0, c).start()
+        copy(below, 2, c).start()
+        if t < 4:
+            above = lax.rem(y + t, NY)
+            copy(above, 1, c).wait_recv()
+            if t < 3:
+                copy(above, 1, c).start()
+            copy(above, 2, c).start()
+
+    def step_sent(t, copy):
+        below = lax.rem(y + NY - t, NY)
+        if t < 4:
+            copy(below, 0, c).wait_send()
+        copy(below, 2, c).wait_send()
+        if t < 4:
+            above = lax.rem(y + t, NY)
+            if t < 3:
+                copy(above, 1, c).wait_send()
+            copy(above, 2, c).wait_send()
+
     xcopy(y, 0, c).start()
     xcopy(y, 1, c).start()
 
     lane = lax.broadcasted_iota(jnp.int32, (128, 256), 1)
     image = lax.broadcasted_iota(jnp.int32, (128, 256), 0) // 64
-    for s in range(SAMPLES):
+    def mask(micro, s):
         seen = jnp.where(
             lane < 128,
-            jnp.where(lane < 64, visible[p, s, 0], visible[p, s, 1]),
-            jnp.where(lane < 192, visible[p, s, 2], visible[p, s, 3]),
-        )
-        bias[s] = jnp.where(seen == image, 0.0, -1e30).astype(F32)
+            jnp.where(lane < 64, visible[micro, s, 0], visible[micro, s, 1]),
+            jnp.where(lane < 192, visible[micro, s, 2], visible[micro, s, 3]),
+        )
+        return jnp.where(seen == image, 0.0, -1e30).astype(F32)
+
+    for s in range(SAMPLES):
+        bias[s] = mask(p, s)
+        bias2[s] = mask(mate // NY, s)
     acc[...] = jnp.zeros_like(acc)
 
+    @pl.when(inner)
+    def _():
+        more[...] = jnp.zeros_like(more)
+        lend(0).wait_recv()
+        for to in range(3):
+            xcopy2(y, to, c).start()
+
     for t in range(1, 5):
-        below = lax.rem(y + NY - t, NY)
-        xcopy(below, 0, c).wait_recv()
+        step(t, xcopy)
+
+        @pl.when(inner)
+        def _():
+            step(t, xcopy2)
+
         if t < 4:
-            xcopy(below, 0, c).start()
-        xcopy(below, 2, c).start()
-        if t < 4:
-            above = lax.rem(y + t, NY)
-            xcopy(above, 1, c).wait_recv()
-            if t < 3:
-                xcopy(above, 1, c).start()
-            xcopy(above, 2, c).start()
-        relay(1, t - 1)
+            relay(1, t - 1, inner)
+        else:
+            relay_sides(1, t - 1, p == 1, p == 2)
+        if t > 1:
+            relay(1, t - 1, end)
     for t in range(1, NY):
         source = lax.rem(y + t, NY)
         xcopy(source, 2, 1 - c).wait_recv()
     factor = jnp.tanh(jnp.full((1, HD), gate[y], F32))
 
+    own = (qbuf, gbuf, abuf, bias)
+    lent = (qbuf2, gbuf2, abuf2, bias2)
+
     def ready(h):
         for d in range(2, NZ):
-            relay(d, h)
+            relay(d, h, end)
         local_q(h).wait()
         local_g(h).wait()
-        kvbuf[...] = nn(xbuf[...], wbuf[h]).astype(BF16)
-
-    def attend(h, s):
+        project(h, xbuf)
+
+    def project(h, tokens):
+        kvbuf[...] = nn(tokens[...], wbuf[h]).astype(BF16)
+
+    def attend(h, s, arrays=own):
+        query_ref, cot_ref, att_ref, bias_ref = arrays
         image_rows = pl.ds(pl.multiple_of(s * 128, 128), 128)
         text_rows = pl.ds(pl.multiple_of(s * 256, 256), 256)
         keys = kvbuf[image_rows, :HD]
         values = kvbuf[image_rows, HD:]
-        qs = qbuf[h, text_rows]
-        hg = (factor * gbuf[h, text_rows].astype(F32)).astype(BF16)
-        e = jnp.exp(nt(keys, qs) * SCALE + bias[s])
+        qs = query_ref[h, text_rows]
+        hg = (factor * cot_ref[h, text_rows].astype(F32)).astype(BF16)
+        e = jnp.exp(nt(keys, qs) * SCALE + bias_ref[s])
         total = jnp.sum(e, axis=0, keepdims=True)
         probs = e * (1.0 / jnp.where(total > 0.0, total, 1.0))
         probs_b = probs.astype(BF16)
-        abuf[h, text_rows] = (factor * tn(probs_b, values)).astype(BF16)
+        att_ref[h, text_rows] = (factor * tn(probs_b, values)).astype(BF16)
         dkv[image_rows, HD:] = nn(probs_b, hg).astype(BF16)
         pg = nt(values, hg)
         delta = jnp.sum(probs * pg, axis=0, keepdims=True)
         sg = (probs * (pg - delta) * SCALE).astype(BF16)
         dkv[image_rows, :HD] = nn(sg, qs).astype(BF16)
 
-    def one_head(h, carry):
+    def out_copy(h):
+        return pltpu.make_async_copy(abuf.at[h], att_out.at[0, :, pl.ds(h * HD, HD)], lo.at[h])
+
+    place, peers = (section, p, y, x, c), (sib, partner, at_y, at_x)
+    reduce = reduction(acc, bufs, sems, place, peers)
+    reduce2 = reduction(acc2, bufs2, sems2, place, peers)
+
+    relay(2, 0, inner)
+    relay(2, 1, inner)
+
+    @pl.when(inner)
+    def _():
+        for t in range(NY):
+            xcopy2(lax.rem(y + t, NY), 2, 1 - c).wait_recv()
+        lend(1).wait_recv()
+        lend(2).wait_recv()
+        project(0, xbuf2)
+        for s in range(SAMPLES):
+            attend(0, s, lent)
+        give_back().start()
+        acc2[...] = nt(dkv[...], wbuf[0])
+        for k in range(SAMPLES):
+            reduce2["pair"](k)
+
+    relay(2, 2, inner)
+    relay_sides(1, HEADS - 1, p == 2, p == 1)
+
+    @pl.when(inner)
+    def _():
+        project(0, xbuf)
+        for s in range(SAMPLES):
+            attend(0, s)
+        out_copy(0).start()
+        acc[...] += nt(dkv[...], wbuf[0])
+
+    relay(2, HEADS - 1, inner)
+
+    for h in range(1, HEADS - 1):
         ready(h)
         for s in range(SAMPLES):
             attend(h, s)
         out_copy(h).start()
         acc[...] += nt(dkv[...], wbuf[h])
-        return carry
-
-    def out_copy(h):
-        return pltpu.make_async_copy(abuf.at[h], att_out.at[0, :, pl.ds(h * HD, HD)], lo.at[h])
-
-    lax.fori_loop(0, HEADS - 1, one_head, 0)
-
-    reduce = reduction(acc, bufs, sems, (section, p, y, x, c), (sib, partner, at_y, at_x))
+
+        @pl.when(inner)
+        def _():
+            for k in range(SAMPLES):
+                reduce2["along_x" if h == 1 else "along_y"](k)
+
     ready(HEADS - 1)
     for k in range(SAMPLES):
         s = sample_at(y, k)
@@ -365,9 +500,25 @@
             reduce["along_x"](k - 1)
     reduce["along_x"](SAMPLES - 1)
     out_copy(HEADS - 1).start()
+
+    @pl.when(inner)
+    def _():
+        mine2[...] = reduce2["owned"]().astype(BF16)
+        give_sum().start()
+
+    @pl.when(end)
+    def _():
+        give_back().wait_recv()
+        out_copy(0).start()
+
     for k in range(SAMPLES):
         reduce["along_y"](k)
-    reduce["planes"]()
+
+    @pl.when(end)
+    def _():
+        give_sum().wait_recv()
+
+    reduce["planes"](more)
     reduce["spread"]()
     reduce["collect"](obuf)
     last = pltpu.make_async_copy(obuf, vis_out, lsem.at[1])
@@ -375,27 +526,37 @@
 
     for h in range(HEADS):
         for q in range(NZ):
-
-            @pl.when(jnp.logical_and(has_left, p <= q))
+            from_right = jnp.logical_and(send_left(h), p <= q)
+            from_left = jnp.logical_and(send_right(h), p >= q)
+
+            @pl.when(from_right)
             def _():
                 zcopy(q, h, 0).wait_send()
 
-            @pl.when(jnp.logical_and(has_right, p >= q))
+            @pl.when(from_left)
             def _():
                 zcopy(q, h, 1).wait_send()
 
     xcopy(y, 0, c).wait_send()
     xcopy(y, 1, c).wait_send()
     for t in range(1, 5):
-        below = lax.rem(y + NY - t, NY)
-        if t < 4:
-            xcopy(below, 0, c).wait_send()
-        xcopy(below, 2, c).wait_send()
-        if t < 4:
-            above = lax.rem(y + t, NY)
-            if t < 3:
-                xcopy(above, 1, c).wait_send()
-            xcopy(above, 2, c).wait_send()
+        step_sent(t, xcopy)
+
+    @pl.when(inner)
+    def _():
+        for to in range(3):
+            xcopy2(y, to, c).wait_send()
+        for t in range(1, 5):
+            step_sent(t, xcopy2)
+        give_back().wait_send()
+        give_sum().wait_send()
+        reduce2["shared_sent"]()
+
+    @pl.when(end)
+    def _():
+        for i in range(3):
+            lend(i).wait_send()
+
     reduce["sent"]()
     for h in range(HEADS):
         out_copy(h).wait()
@@ -424,7 +585,16 @@
             pltpu.VMEM((VT, 2 * HD), BF16),
             pltpu.VMEM((VT, 2 * HD), BF16),
             pltpu.VMEM((VT, DV), F32),
+            pltpu.VMEM((VT, DV), BF16),
+            pltpu.VMEM((1, 1024, HD), BF16),
+            pltpu.VMEM((1, 1024, HD), BF16),
+            pltpu.VMEM((1, 1024, HD), BF16),
+            pltpu.VMEM((SAMPLES, 128, 256), F32),
+            pltpu.VMEM((VT, DV), F32),
+            pltpu.VMEM((16, SHARE), BF16),
+            pltpu.VMEM((16, SHARE), BF16),
             pltpu.VMEM((64, DV), BF16),
+            reduction_bufs(),
             reduction_bufs(),
             dma((2,)),
             dma((HEADS, 2)),
@@ -433,9 +603,11 @@
             dma((HEADS,)),
             dma((2, NZ, HEADS)),
             dma((NZ, HEADS)),
-            dma((3, NY)),
-            dma((NY,)),
-            dma((NY,)),
+            [dma((3, NY)), dma((NY,)), dma((NY,))],
+            [dma((3, NY)), dma((NY,)), dma((NY,))],
+            dma((5,)),
+            dma((5,)),
+            reduction_sems(),
             reduction_sems(),
         ],
         compiler_params=pltpu.CompilerParams(

time: 106 us -> 103 us (0.972)
  Pallas kernels: 102 us -> 98.5 us
    pallas_call x1, Pallas kernels: 102 us -> 98.5 us  [shards(): pl.pallas_call(kernel, out_shape=(jax.ShapeDtypeStruct(queries.shape, BF1...]
where the time goes in v3:
time: 103 us; the launch traced here: 102 us
  Pallas kernels  98.5 us (96%)
  local copies, waits for them, and re-layouts  2.99 us (3%)
    pallas_call x1, Pallas kernels, shards(): pl.pallas_call(kernel, out_shape=(jax.ShapeDtypeStruct(queries.shape, BF1...  98.5 us
    unnamed x4, local copies, waits for them, and re-layouts  2.99 us

profile of v3, /device:TPU:1, one launch (start us, length us, event | category | flops | bytes accessed | tf_op | source)
XLA Modules:
  0.0 102.1 jit_solution(16954549008655922150)
XLA Ops:
  0.6 98.5 %shard_map.86 = (bf16[1,1024,512]{2,1,0:T(8,128)(2,1)}, bf16[64,1664]{1,0:T(8,128)(2,1)}) custom-call(f32[8]{0:T(128)} %gate.1, s32[4,4,4]{2,1,0:T(4,128)} %visible.1, bf16[64,1664]{1,0:T(8,128)(2,1)} %vision.1, bf16[416,512]{1,0:T(8,128)(2,1)} %wk.1, bf16[416,512]{1,0:T(8,128)(2,1)} %wv.1, bf16[1,1024,512]{2,1,0:T(8,128)(2,1)} %query.1, ...), custom_call_target="tpu_custom_call" | custom-call | flops 4000000000 | bytes 5000000 | tf_op jit(solution)/shard_map/pallas_call | solution.py:570
  99.1 0.0 copy-start
  99.2 2.3 %copy.11 = bf16[1,1024,512]{2,1,0:T(8,128)(2,1)} copy(bf16[1,1024,512]{2,1,0:T(8,128)(2,1)} %get-tuple-element.4) | data formatting | bytes 2097152
  101.5 0.0 copy-done
  101.5 0.7 copy.12
Async XLA Ops:
  99.1 2.3 %copy-start = (bf16[64,1664]{1,0:T(8,128)(2,1)S(1)}, bf16[64,1664]{1,0:T(8,128)(2,1)}, u32[]{:S(2)}) copy-start(bf16[64,1664]{1,0:T(8,128)(2,1)} %get-tuple-element.5) | copy-start | bytes 638980

commit v4 on v3

--- a/solution.py
+++ b/solution.py
@@ -392,15 +392,15 @@
 
     for t in range(1, 5):
         step(t, xcopy)
-
-        @pl.when(inner)
-        def _():
-            step(t, xcopy2)
-
         if t < 4:
             relay(1, t - 1, inner)
         else:
             relay_sides(1, t - 1, p == 1, p == 2)
+
+        @pl.when(inner)
+        def _():
+            step(t, xcopy2)
+
         if t > 1:
             relay(1, t - 1, end)
     for t in range(1, NY):
@@ -469,6 +469,8 @@
 
     @pl.when(inner)
     def _():
+        for k in range(SAMPLES):
+            reduce2["along_x"](k)
         project(0, xbuf)
         for s in range(SAMPLES):
             attend(0, s)
@@ -484,10 +486,12 @@
         out_copy(h).start()
         acc[...] += nt(dkv[...], wbuf[h])
 
-        @pl.when(inner)
-        def _():
-            for k in range(SAMPLES):
-                reduce2["along_x" if h == 1 else "along_y"](k)
+        if h == HEADS - 2:
+
+            @pl.when(inner)
+            def _():
+                for k in range(SAMPLES):
+                    reduce2["along_y"](k)
 
     ready(HEADS - 1)
     for k in range(SAMPLES):

time: 103 us -> 101 us (0.981); the launches traced: 102 us -> 101 us
  no operation moved by 1% of the time
where the time goes in v4:
time: 101 us
  Pallas kernels  97.7 us (97%)
  local copies, waits for them, and re-layouts  2.99 us (3%)
    pallas_call x1, Pallas kernels, shards(): pl.pallas_call(kernel, out_shape=(jax.ShapeDtypeStruct(queries.shape, BF1...  97.7 us
    unnamed x4, local copies, waits for them, and re-layouts  2.99 us

profile of v4, /device:TPU:1, one launch (start us, length us, event | category | flops | bytes accessed | tf_op | source)
XLA Modules:
  0.0 101.3 jit_solution(15042037667428737483)
XLA Ops:
  0.6 97.7 %shard_map.86 = (bf16[1,1024,512]{2,1,0:T(8,128)(2,1)}, bf16[64,1664]{1,0:T(8,128)(2,1)}) custom-call(f32[8]{0:T(128)} %gate.1, s32[4,4,4]{2,1,0:T(4,128)} %visible.1, bf16[64,1664]{1,0:T(8,128)(2,1)} %vision.1, bf16[416,512]{1,0:T(8,128)(2,1)} %wk.1, bf16[416,512]{1,0:T(8,128)(2,1)} %wv.1, bf16[1,1024,512]{2,1,0:T(8,128)(2,1)} %query.1, ...), custom_call_target="tpu_custom_call" | custom-call | flops 4000000000 | bytes 5000000 | tf_op jit(solution)/shard_map/pallas_call | solution.py:574
  98.3 0.0 copy-start
  98.3 2.3 %copy.11 = bf16[1,1024,512]{2,1,0:T(8,128)(2,1)} copy(bf16[1,1024,512]{2,1,0:T(8,128)(2,1)} %get-tuple-element.4) | data formatting | bytes 2097152
  100.6 0.0 copy-done
  100.6 0.7 copy.12
Async XLA Ops:
  98.3 2.3 %copy-start = (bf16[64,1664]{1,0:T(8,128)(2,1)S(1)}, bf16[64,1664]{1,0:T(8,128)(2,1)}, u32[]{:S(2)}) copy-start(bf16[64,1664]{1,0:T(8,128)(2,1)} %get-tuple-element.5) | copy-start | bytes 638980

commit v5 on v4

--- a/solution.py
+++ b/solution.py
@@ -459,7 +459,6 @@
         project(0, xbuf2)
         for s in range(SAMPLES):
             attend(0, s, lent)
-        give_back().start()
         acc2[...] = nt(dkv[...], wbuf[0])
         for k in range(SAMPLES):
             reduce2["pair"](k)
@@ -478,6 +477,10 @@
         acc[...] += nt(dkv[...], wbuf[0])
 
     relay(2, HEADS - 1, inner)
+
+    @pl.when(inner)
+    def _():
+        give_back().start()
 
     for h in range(1, HEADS - 1):
         ready(h)
@@ -510,19 +513,20 @@
         mine2[...] = reduce2["owned"]().astype(BF16)
         give_sum().start()
 
+    for k in range(SAMPLES):
+        reduce["along_y"](k)
+
+    @pl.when(end)
+    def _():
+        give_sum().wait_recv()
+
+    reduce["planes"](more)
+
     @pl.when(end)
     def _():
         give_back().wait_recv()
         out_copy(0).start()
 
-    for k in range(SAMPLES):
-        reduce["along_y"](k)
-
-    @pl.when(end)
-    def _():
-        give_sum().wait_recv()
-
-    reduce["planes"](more)
     reduce["spread"]()
     reduce["collect"](obuf)
     last = pltpu.make_async_copy(obuf, vis_out, lsem.at[1])

time: 101 us -> 97.1 us (0.961)
  Pallas kernels: 97.7 us -> 93.3 us
    pallas_call x1, Pallas kernels: 97.7 us -> 93.3 us  [shards(): pl.pallas_call(kernel, out_shape=(jax.ShapeDtypeStruct(queries.shape, BF1...]
where the time goes in v5:
time: 97.1 us; the launch traced here: 96.9 us
  Pallas kernels  93.3 us (96%)
  local copies, waits for them, and re-layouts  2.99 us (3%)
    pallas_call x1, Pallas kernels, shards(): pl.pallas_call(kernel, out_shape=(jax.ShapeDtypeStruct(queries.shape, BF1...  93.3 us
    unnamed x4, local copies, waits for them, and re-layouts  2.99 us

profile of v5, /device:TPU:1, one launch (start us, length us, event | category | flops | bytes accessed | tf_op | source)
XLA Modules:
  0.0 96.9 jit_solution(3838635276094795630)
XLA Ops:
  0.6 93.3 %shard_map.86 = (bf16[1,1024,512]{2,1,0:T(8,128)(2,1)}, bf16[64,1664]{1,0:T(8,128)(2,1)}) custom-call(f32[8]{0:T(128)} %gate.1, s32[4,4,4]{2,1,0:T(4,128)} %visible.1, bf16[64,1664]{1,0:T(8,128)(2,1)} %vision.1, bf16[416,512]{1,0:T(8,128)(2,1)} %wk.1, bf16[416,512]{1,0:T(8,128)(2,1)} %wv.1, bf16[1,1024,512]{2,1,0:T(8,128)(2,1)} %query.1, ...), custom_call_target="tpu_custom_call" | custom-call | flops 4000000000 | bytes 5000000 | tf_op jit(solution)/shard_map/pallas_call | solution.py:578
  93.9 0.0 copy-start
  93.9 2.3 %copy.11 = bf16[1,1024,512]{2,1,0:T(8,128)(2,1)} copy(bf16[1,1024,512]{2,1,0:T(8,128)(2,1)} %get-tuple-element.4) | data formatting | bytes 2097152
  96.2 0.0 copy-done
  96.2 0.7 copy.12
Async XLA Ops:
  93.9 2.3 %copy-start = (bf16[64,1664]{1,0:T(8,128)(2,1)S(1)}, bf16[64,1664]{1,0:T(8,128)(2,1)}, u32[]{:S(2)}) copy-start(bf16[64,1664]{1,0:T(8,128)(2,1)} %get-tuple-element.5) | copy-start | bytes 638980
